TPU v7x, 32 devices: a whole 2x2x4 slice. The times are simulated.
32 devices in a mesh: groups: 2 (over x), beam: 8 (over z, y), sub: 2 (over core).
Axes of the slice: x: 2, y: 2, z: 4, core: 2. Of those that a mesh axis runs over, the one named last changes fastest.
Arguments:
- intensities: bfloat16 [32, 16384, 270], P('groups', ('beam', 'sub')), parts along dimension 0, may hold values from -0.046875 to 0.046875
- sweep_delays: int32 [16384, 16], replicated, may hold values from 0 to 7
- band_offsets: int32 [16, 1024], replicated, may hold values from 0 to 7
- coarse_trial: int32 [1024], replicated, may hold values from 0 to 15
Outputs:
- dm_planes: float32 [1024, 32, 256], P('sub', ('groups', 'beam')), parts along dimension 1
There are 2 independent parts, one for each index of `groups`. A program takes and returns all parts, laid end to end along the dimension named above; an argument that names none is the same for every part. Nothing has to cross between parts.
All inputs are finite; a program needn't handle non-finite values.
Results may differ from a plain program's by a relative error of at most 0.0029.
Values may be sent and summed in bfloat16 or wider, within the bound.
A program may use at most 128 MiB of HBM per device.

v0:
```python
import jax
import jax.numpy as jnp
from jax import lax
from jax.sharding import PartitionSpec as P

CHANNELS = 16384
SUBBANDS = 16
COARSE = 16
BAND_LAGS = 8
SUB_LAGS = 8


def section_one(intens, delays, bands, span_out, groups):
    count_beams, chans, span = intens.shape
    block = min(chans, 1024)
    cols = groups * COARSE
    members = jnp.arange(groups, dtype=jnp.int32)
    lag_ids = jnp.arange(BAND_LAGS, dtype=jnp.int32)

    def add_block(index, total):
        member = bands[:, None] == members[None, :]
        lag_hit = delays[:, None, :] == lag_ids[None, :, None]
        table = (
            (member[:, None, :, None] & lag_hit[:, :, None, :])
            .reshape(block, BAND_LAGS * cols)
            .astype(jnp.bfloat16)
        )
        return total + jnp.einsum("bct,cn->btn", intens, table, preferred_element_type=jnp.float32)

    empty = jnp.zeros((count_beams, span, BAND_LAGS * cols), jnp.float32)
    spread = lax.fori_loop(0, chans // block, add_block, empty)
    result = spread[:, 0:span_out, 0:cols]
    for lag in range(1, BAND_LAGS):
        result = result + spread[:, lag : lag + span_out, lag * cols : (lag + 1) * cols]
    return result


def section_two(planes, offsets, coarse_map, count):
    halves_here, beams_here, span_out, cols = planes.shape
    samples = span_out - SUB_LAGS + 1
    coarse_hit = coarse_map[None, :] == jnp.arange(COARSE, dtype=jnp.int32)[:, None]
    total = jnp.zeros((count, beams_here, samples), jnp.float32)
    for lag in range(SUB_LAGS):
        table = (
            ((offsets == lag)[:, None, :] & coarse_hit[None, :, :])
            .reshape(cols, count)
            .astype(jnp.bfloat16)
        )
        total = total + jnp.einsum(
            "hbtn,nm->mbt",
            planes[:, :, lag : lag + samples, :],
            table,
            preferred_element_type=jnp.float32,
        )
    return total


def on_device(intensities, sweep_delays, band_offsets, coarse_trial):
    beams_all, chans_local, span = intensities.shape
    beam_count = lax.axis_size("beam")
    sub_count = lax.axis_size("sub")
    per_device = beams_all // beam_count
    out_len = span - BAND_LAGS + 1
    trials_local = band_offsets.shape[1] // sub_count
    sub_width = CHANNELS // SUBBANDS
    sub_here = lax.axis_index("sub")
    held = max(1, chans_local // sub_width)
    first = (lax.axis_index("beam") * sub_count + sub_here) * chans_local
    delay_view = lax.dynamic_slice_in_dim(sweep_delays, first, chans_local, 0)
    band_view = (first + jnp.arange(chans_local, dtype=jnp.int32)) // sub_width - first // sub_width
    local_terms = section_one(intensities, delay_view, band_view, out_len, held)
    grouped = local_terms.reshape(beam_count, per_device, out_len, held * COARSE)
    arrived = lax.all_to_all(grouped, "beam", split_axis=0, concat_axis=0, tiled=True)
    arrived = arrived.reshape(beam_count, per_device, out_len, held, COARSE)
    source_first = (
        (jnp.arange(beam_count, dtype=jnp.int32) * sub_count + sub_here) * chans_local // sub_width
    )
    target = source_first[:, None] + jnp.arange(held, dtype=jnp.int32)[None, :]
    placing = (target[:, :, None] == jnp.arange(SUBBANDS, dtype=jnp.int32)[None, None, :]).astype(
        jnp.float32
    )
    planes = jnp.einsum(
        "ibtpc,ips->btsc", arrived, placing, precision=lax.Precision.HIGHEST
    ).reshape(per_device, out_len, SUBBANDS * COARSE)
    rounded = planes.astype(jnp.bfloat16)
    return lax.psum_scatter(
        section_two(rounded[None], band_offsets, coarse_trial, lax.axis_size("sub") * trials_local),
        "sub",
        scatter_dimension=0,
        tiled=True,
    )


def solution(mesh):
    in_specs = (P("groups", ("beam", "sub"), None), P(), P(), P())
    out_specs = P("sub", ("groups", "beam"), None)
    return jax.shard_map(
        on_device, mesh=mesh, in_specs=in_specs, out_specs=out_specs, check_vma=False
    )
```

profile of v0, /device:TPU:0, one launch (start us, length us, event | category | flops | bytes accessed | tf_op | source)
XLA Modules:
  0.0 73.1 jit_solution(8438088615132237709)
XLA Ops:
  6.5 0.0 copy-start
  6.6 0.1 eq.135
  6.6 1.1 %copy-done = s32[16384,16]{0,1:T(8,128)S(1)} copy-done((s32[16384,16]{0,1:T(8,128)S(1)}, s32[16384,16]{0,1:T(8,128)}, u32[]{:S(2)}) %copy-start) | copy-done | bytes 1048600
  7.8 0.2 fusion.6
  7.9 13.4 %fusion.2 = f32[16,270,128]{2,1,0:T(8,128)S(1)} fusion(bf16[16,1024,270]{1,0,2:T(8,128)(2,1)} %param.4, pred[1024,128]{0,1:T(32,128)(4,1)S(1)} %fusion.6), kind=kOutput, calls=%fused_computation.10 | convolution fusion | flops 1132462080 | bytes 11190272 | tf_op jit(solution)/shard_map/while/body/eval_jaxpr/bct,cn->btn/dot_general | solution.py:28
  21.3 4.1 %slice_add_fusion = f32[16,263,16]{2,1,0:T(8,128)S(1)} fusion(f32[16,270,128]{2,1,0:T(8,128)S(1)} %fusion.2), kind=kLoop, calls=%fused_computation.2 | loop fusion | flops 471296 | bytes 2423808 | tf_op jit(solution)/shard_map/add | solution.py:34
  25.5 0.0 copy-start.5
  25.5 0.0 copy-start.6
  25.5 1.6 %copy.40 = f32[8,2,263,16]{2,3,1,0:T(8,128)} copy(f32[8,2,263,16]{3,2,1,0:T(8,128)S(1)} %bitcast.100) | data formatting | bytes 538624 | tf_op jit(solution)/shard_map/reshape | solution.py:72
  27.1 7.3 %all-to-all-start = ((f32[8,2,263,16]{2,3,1,0:T(8,128)}), f32[8,2,263,16]{2,3,1,0:T(8,128)S(1)}, u32[]{:S(2)}, u32[]{:S(2)}) async-start(f32[8,2,263,16]{2,3,1,0:T(8,128)} %copy.40), calls=%async_computation | async-start | bytes 786432 | tf_op jit(solution)/shard_map/all_to_all | solution.py:73
  34.4 0.0 reduce-scatter.2.cloned.1.call-start
  34.4 0.0 copy-done.5
  34.4 0.1 broadcast_compare_fusion
  34.5 0.0 copy-done.6
  34.6 1.2 %broadcast_and_fusion = (pred[16,16,1024]{2,1,0:T(8,128)(4,1)S(1)}, pred[16,16,1024]{2,1,0:T(8,128)(4,1)S(1)}, pred[16,16,1024]{2,1,0:T(8,128)(4,1)S(1)}, pred[1...) fusion(pred[16,1024]{1,0:T(8,128)(4,1)S(1)} %get-tuple-element., ...), kind=kLoop, calls=%fused_computation.24 | loop fusion | flops 2097152 | bytes 2244608 | tf_op jit(solution)/shard_map/and | solution.py:45
  35.8 0.9 %bitcast_convert_fusion.7 = bf16[256,1024,1]{1,0,2:T(8,128)(2,1)} fusion(pred[16,16,1024]{2,1,0:T(8,128)(4,1)S(1)} %get-tuple-element.38), kind=kLoop, calls=%fused_computation.20 | loop fusion | flops 262144 | bytes 786432
  36.6 0.2 bitcast_convert_fusion.3
  36.8 1.1 %bitcast_convert_fusion.5 = (bf16[256,1024,1]{1,0,2:T(8,128)(2,1)}, bf16[256,1024,1]{1,0,2:T(8,128)(2,1)S(1)}) fusion(pred[16,16,1024]{2,1,0:T(8,128)(4,1)S(1)} %get-tuple-element.33, pred[16,16,1024]{2,1,0:T(8,128)(4,1)S(1)} %get-tuple-element.32), kind=kLoop, calls=%fused_computation.18 | loop fusion | flops 524288 | bytes 1572864
  37.9 0.1 bitcast_convert_fusion
  38.0 1.2 %bitcast_convert_fusion.1 = (bf16[256,1024,1]{1,0,2:T(8,128)(2,1)}, bf16[256,1024,1]{1,0,2:T(8,128)(2,1)}) fusion(pred[16,16,1024]{2,1,0:T(8,128)(4,1)S(1)} %get-tuple-element.37, pred[16,16,1024]{2,1,0:T(8,128)(4,1)S(1)} %get-tuple-element.36), kind=kLoop, calls=%fused_computation.14 | loop fusion | flops 524288 | bytes 1572864
  39.2 6.9 %all-to-all-done = f32[8,2,263,16]{2,3,1,0:T(8,128)S(1)} async-done(((f32[8,2,263,16]{2,3,1,0:T(8,128)}), f32[8,2,263,16]{2,3,1,0:T(8,128)S(1)}, u32[]{:S(2)}, u32[]{:S(2)}) %all-to-all-start) | async-done | bytes 269344 | tf_op jit(solution)/shard_map/all_to_all | solution.py:73
  46.1 0.7 fusion.5
  46.8 0.1 copy.42
  46.9 0.5 fusion.11
  47.4 0.0 copy-start.1
  47.4 0.5 fusion.12
  48.0 0.5 copy-done.1
  48.4 0.5 fusion.13
  49.0 0.0 copy-start.3
  49.0 0.5 fusion.14
  49.5 0.0 copy-start.2
  49.6 0.5 copy-done.3
  50.0 0.5 fusion.10
  50.6 0.0 copy-start.4
  50.6 0.0 copy-done.2
  50.6 0.5 fusion.9
  51.2 0.5 copy-done.4
  51.6 0.5 fusion.15
  52.1 2.3 %add_add_fusion = f32[1024,2,256]{2,0,1:T(8,128)} fusion(f32[1024,2,256]{2,0,1:T(8,128)S(1)} %fusion.9, f32[1024,2,256]{2,0,1:T(8,128)S(1)} %fusion.10, f32[1024,2,256]{2,0,1:T(8,128)S(1)} %fusion.11, f32[1024,2,256]{2,0,1:T(8,128)S(1)} %fusion.12, f32[1024,2,256]{2,0,1:T(8,128)S(1)} %fusion.13, f32[1024,2,256]{2,0,1:T(8,128)S(1)} %fusion.15, ...), kind=kOutput, calls=%fused_computation.9 | convolution fusion | flops 272105472 | bytes 17563648 | tf_op jit(solution)/shard_map/hbtn,nm->mbt/dot_general | solution.py:49
  54.4 0.0 reduce-scatter.2.cloned.1.call-update
  54.4 8.8 %reduce-scatter.2.cloned.1.call-done = f32[512,2,256]{2,0,1:T(8,128)} async-done(((f32[1024,2,256]{2,0,1:T(8,128)}), f32[512,2,256]{2,0,1:T(8,128)}) %reduce-scatter.2.cloned.1.call-update) | async-done | bytes 1048592 | tf_op jit(solution)/shard_map/reduce_scatter | solution.py:86
  63.2 3.0 %copy.59 = f32[512,2,256]{2,1,0:T(2,128)} copy(f32[512,2,256]{2,0,1:T(8,128)} %reduce-scatter.2.cloned.1.call-done) | data formatting | bytes 2097152 | tf_op jit(solution)/shard_map/reduce_scatter | solution.py:86
  (5 shorter events, 0.0 us)
Async XLA Ops:
  6.5 1.2 %copy-start = (s32[16384,16]{0,1:T(8,128)S(1)}, s32[16384,16]{0,1:T(8,128)}, u32[]{:S(2)}) copy-start(s32[16384,16]{0,1:T(8,128)} %param.5) | copy-start | bytes 3145732
  25.5 9.0 %copy-start.5 = (s32[16,1024]{1,0:T(8,128)S(1)}, s32[16,1024]{1,0:T(8,128)}, u32[]{:S(2)}) copy-start(s32[16,1024]{1,0:T(8,128)} %param.6) | copy-start | bytes 196612
  25.5 9.1 %copy-start.6 = (s32[1024]{0:T(1024)S(1)}, s32[1024]{0:T(1024)}, u32[]{:S(2)}) copy-start(s32[1024]{0:T(1024)} %param.7) | copy-start | bytes 12292
  27.1 19.0 %all-to-all-start = ((f32[8,2,263,16]{2,3,1,0:T(8,128)}), f32[8,2,263,16]{2,3,1,0:T(8,128)S(1)}, u32[]{:S(2)}, u32[]{:S(2)}) async-start(f32[8,2,263,16]{2,3,1,0:T(8,128)} %copy.40), calls=%async_computation | async-start | bytes 786432 | tf_op jit(solution)/shard_map/all_to_all | solution.py:73
  34.4 28.8 %reduce-scatter.2.cloned.1.call-start = ((), (), s32[]{:S(2)}) async-start(), calls=%async_computation.2 | async-start | bytes 3145728 | tf_op jit(solution)/shard_map/reduce_scatter | solution.py:86
  47.4 1.0 %copy-start.1 = (bf16[256,1024,1]{1,0,2:T(8,128)(2,1)S(1)}, bf16[256,1024,1]{1,0,2:T(8,128)(2,1)}, u32[]{:S(2)}) copy-start(bf16[256,1024,1]{1,0,2:T(8,128)(2,1)} %get-tuple-element.43) | copy-start | bytes 1572868
  49.0 1.0 %copy-start.3 = (bf16[256,1024,1]{1,0,2:T(8,128)(2,1)S(1)}, bf16[256,1024,1]{1,0,2:T(8,128)(2,1)}, u32[]{:S(2)}) copy-start(bf16[256,1024,1]{1,0,2:T(8,128)(2,1)} %get-tuple-element.40) | copy-start | bytes 1572868
  49.5 1.1 %copy-start.2 = (bf16[256,1024,1]{1,0,2:T(8,128)(2,1)S(1)}, bf16[256,1024,1]{1,0,2:T(8,128)(2,1)}, u32[]{:S(2)}) copy-start(bf16[256,1024,1]{1,0,2:T(8,128)(2,1)} %get-tuple-element.39) | copy-start | bytes 1572868
  50.6 1.1 %copy-start.4 = (bf16[256,1024,1]{1,0,2:T(8,128)(2,1)S(1)}, bf16[256,1024,1]{1,0,2:T(8,128)(2,1)}, u32[]{:S(2)}) copy-start(bf16[256,1024,1]{1,0,2:T(8,128)(2,1)} %bitcast_convert_fusion.7) | copy-start | bytes 1572868
Sparse Core Ops, SparseCore 0:
  54.5 8.6 reduce-scatter.1
where the time goes:
time: 73.5 us; the launch traced here: 73.1 us
  matrix products  20.1 us (27%)
  waiting for transfers between devices  15.7 us (21%)
  between operations  13.6 us (19%)
  other arithmetic  8.99 us (12%)
  local copies, waits for them, and re-layouts  7.37 us (10%)
  starting transfers between devices  7.32 us (10%)
    dot_general x1, matrix products, add_block(): jnp.einsum('bct,cn->btn', intens, table, preferred_element_type=jnp.float32)  13.4 us
    reduce_scatter x1, waiting for transfers between devices, on_device(): lax.psum_scatter(section_two(rounded[None], band_offsets, coarse_trial, l...  8.82 us
    all_to_all x1, starting transfers between devices, on_device(): lax.all_to_all(grouped, 'beam', split_axis=0, concat_axis=0, tiled=True)  7.28 us
    all_to_all x1, waiting for transfers between devices, on_device(): lax.all_to_all(grouped, 'beam', split_axis=0, concat_axis=0, tiled=True)  6.9 us
    dot_general x8, matrix products, section_two(): jnp.einsum('hbtn,nm->mbt', planes[:, :, lag:lag + samples, :], table, pre...  5.99 us
    add x1, other arithmetic, section_one(): result = result + spread[:, lag:lag + span_out, lag * cols:(lag + 1) * cols]  4.15 us
    unnamed x5, other arithmetic  3.39 us
    reduce_scatter x1, local copies, waits for them, and re-layouts, on_device(): lax.psum_scatter(section_two(rounded[None], band_offsets, coarse_trial, l...  3 us
  transfers between devices with their start and end apart: 2, of which 2 were waited for; matrix products, arithmetic and copies ran while one was open for 6% of the time, Pallas kernels for 0%

commit v1 on v0

--- a/solution.py
+++ b/solution.py
@@ -1,6 +1,8 @@
 import jax
 import jax.numpy as jnp
 from jax import lax
+from jax.experimental import pallas as pl
+from jax.experimental.pallas import tpu as pltpu
 from jax.sharding import PartitionSpec as P
 
 CHANNELS = 16384
@@ -91,9 +93,280 @@
     )
 
 
+SAMPLE_LANES = 128
+CHUNK_TIMES = 30
+
+
+def planes_kernel(
+    x_hbm,
+    delays_hbm,
+    offsets_hbm,
+    coarse_hbm,
+    planes_out,
+    key_out,
+    x_vmem,
+    delays_vmem,
+    offsets_vmem,
+    coarse_vmem,
+    table,
+    spread,
+    send,
+    recv,
+    x_sem,
+    small_sem,
+    send_sem,
+    recv_sem,
+    pass_send_sem,
+    pass_recv_sem,
+):
+    span, beams, chans = x_vmem.shape
+    chips = send.shape[0]
+    trials = offsets_vmem.shape[1]
+    chunks = span // CHUNK_TIMES
+    me = lax.axis_index("beam")
+    core = lax.axis_index("sub")
+    mesh_id = pl.DeviceIdType.MESH
+
+    def load_chunk(index):
+        part = pl.ds(index * CHUNK_TIMES, CHUNK_TIMES)
+        return pltpu.make_async_copy(x_hbm.at[part], x_vmem.at[part], x_sem.at[index])
+
+    first = pl.multiple_of((me * 2 + core) * chans, chans)
+    delay_copy = pltpu.make_async_copy(
+        delays_hbm.at[:, pl.ds(first, chans)], delays_vmem, small_sem.at[0]
+    )
+    half = pl.ds(pl.multiple_of(core * trials, trials), trials)
+    offset_copy = pltpu.make_async_copy(offsets_hbm.at[:, half], offsets_vmem, small_sem.at[1])
+    coarse_copy = pltpu.make_async_copy(coarse_hbm.at[:, half], coarse_vmem, small_sem.at[2])
+    delay_copy.start()
+    for index in range(chunks):
+        load_chunk(index).start()
+    offset_copy.start()
+    coarse_copy.start()
+
+    barrier = pltpu.get_barrier_semaphore()
+    for step in range(1, chips):
+        peer = lax.rem(me + step, chips)
+        pl.semaphore_signal(barrier, inc=1, device_id={"beam": peer, "sub": core}, device_id_type=mesh_id)
+    pl.semaphore_signal(barrier, inc=1, device_id={"beam": me, "sub": 1 - core}, device_id_type=mesh_id)
+
+    delay_copy.wait()
+    delays = delays_vmem[...]
+    hits = [(delays == lag).astype(jnp.float32) for lag in range(BAND_LAGS)]
+    table[...] = jnp.concatenate(hits, axis=0).T.astype(jnp.bfloat16)
+    spread[span * beams :, :] = jnp.zeros((spread.shape[0] - span * beams, spread.shape[1]), jnp.float32)
+
+    def multiply(index, carry):
+        load_chunk(index).wait()
+        rows = CHUNK_TIMES * beams
+        block = x_vmem[pl.ds(index * CHUNK_TIMES, CHUNK_TIMES)].reshape(rows, chans)
+        spread[pl.ds(pl.multiple_of(index * rows, rows), rows), :] = jnp.dot(
+            block, table[...], preferred_element_type=jnp.float32
+        )
+        return carry
+
+    lax.fori_loop(0, chunks, multiply, 0)
+
+    def lagged(beam, start, count):
+        lane_lag = lax.broadcasted_iota(jnp.int32, (count, BAND_LAGS * COARSE), 1) // COARSE
+        total = spread[pl.ds(beam + beams * start, count, stride=beams), :]
+        for lag in range(1, BAND_LAGS):
+            later = spread[pl.ds(beam + beams * (start + lag), count, stride=beams), :]
+            total = jnp.where(lane_lag == lag, later, total)
+        return total
+
+    def folded(rows):
+        turned = rows.T
+        total = turned[0:COARSE]
+        for lag in range(1, BAND_LAGS):
+            total = total + turned[lag * COARSE : (lag + 1) * COARSE]
+        return total.astype(jnp.bfloat16)
+
+    def beam_pair(chip):
+        low = chip * 2
+        blocks = []
+        for beam in (low, low + 1):
+            for start in (0, SAMPLE_LANES):
+                blocks.append(folded(lagged(beam, start, SAMPLE_LANES)))
+        ends = [lagged(beam, 2 * SAMPLE_LANES, 8) for beam in (low, low + 1)]
+        ends.append(jnp.zeros((SAMPLE_LANES - 16, BAND_LAGS * COARSE), jnp.float32))
+        blocks.append(folded(jnp.concatenate(ends, axis=0)))
+        return blocks
+
+    def send_copy(step):
+        peer = lax.rem(me + step, chips)
+        return pltpu.make_async_remote_copy(
+            src_ref=send.at[peer],
+            dst_ref=recv.at[me * 2 + core],
+            send_sem=send_sem.at[step],
+            recv_sem=recv_sem.at[me],
+            device_id={"beam": peer, "sub": core},
+            device_id_type=mesh_id,
+        )
+
+    def arrival(source):
+        return pltpu.make_async_remote_copy(
+            src_ref=send.at[source],
+            dst_ref=recv.at[source * 2 + core],
+            send_sem=send_sem.at[0],
+            recv_sem=recv_sem.at[source],
+            device_id={"beam": source, "sub": core},
+            device_id_type=mesh_id,
+        )
+
+    def pass_copy(source, side):
+        slot = recv.at[source * 2 + side]
+        return pltpu.make_async_remote_copy(
+            src_ref=slot,
+            dst_ref=slot,
+            send_sem=pass_send_sem.at[source],
+            recv_sem=pass_recv_sem.at[source],
+            device_id={"beam": me, "sub": 1 - core},
+            device_id_type=mesh_id,
+        )
+
+    pl.semaphore_wait(barrier, chips)
+
+    def send_pair(step, carry):
+        peer = lax.rem(me + step, chips)
+        for index, block in enumerate(beam_pair(peer)):
+            send[peer, index] = block
+        send_copy(step).start()
+        return carry
+
+    lax.fori_loop(1, chips, send_pair, 0)
+    for index, block in enumerate(beam_pair(me)):
+        recv[me * 2 + core, index] = block
+    pass_copy(me, core).start()
+
+    offset_copy.wait()
+    coarse_copy.wait()
+    coarse_ids = lax.broadcasted_iota(jnp.int32, (COARSE, trials), 0)
+    coarse_hit = coarse_ids == coarse_vmem[...]
+    offsets = offsets_vmem[...]
+    keys = [
+        jnp.where(coarse_hit, offsets[sub : sub + 1], -1).astype(jnp.float32)
+        for sub in range(SUBBANDS)
+    ]
+    key_out[...] = jnp.concatenate(keys, axis=0).T.astype(jnp.bfloat16)
+
+    for step in range(1, chips):
+        source = lax.rem(me + chips - step, chips)
+        arrival(source).wait_recv()
+        pass_copy(source, core).start()
+    for step in range(chips):
+        source = lax.rem(me + chips - step, chips)
+        pass_copy(source, 1 - core).wait_recv()
+    for step in range(1, chips):
+        send_copy(step).wait_send()
+    for step in range(chips):
+        source = lax.rem(me + chips - step, chips)
+        pass_copy(source, core).wait_send()
+    planes_out[...] = recv[...]
+
+
+def trials_kernel(planes, key, out, shifted):
+    rows = SUBBANDS * COARSE
+    trials = key.shape[0]
+    samples = 2 * SAMPLE_LANES
+    keys = key[...]
+    one, zero = jnp.bfloat16(1), jnp.bfloat16(0)
+    table = jnp.concatenate(
+        [jnp.where(keys == jnp.bfloat16(lag), one, zero) for lag in range(SUB_LAGS)], axis=1
+    )
+    for beam in range(2):
+        parts = [planes[:, 2 * beam + index].reshape(rows, SAMPLE_LANES) for index in range(2)]
+        end = planes[:, 4].reshape(rows, SAMPLE_LANES)
+        whole = jnp.concatenate(parts + [end], axis=1).astype(jnp.float32)
+        if beam:
+            turned = pltpu.roll(whole[:, samples:], SAMPLE_LANES - 8 * beam, 1)
+            whole = jnp.concatenate([whole[:, :samples], turned], axis=1)
+        for lag in range(SUB_LAGS):
+            moved = whole if lag == 0 else pltpu.roll(whole, whole.shape[1] - lag, 1)
+            shifted[beam, lag * rows : (lag + 1) * rows, :] = moved[:, :samples].astype(jnp.bfloat16)
+        out[:, beam, :] = jnp.dot(table, shifted[beam], preferred_element_type=jnp.float32)
+
+
+def on_device_fused(intensities, sweep_delays, band_offsets, coarse_trial):
+    beams, chans, span = intensities.shape
+    chips = lax.axis_size("beam")
+    trials = band_offsets.shape[1] // 2
+    any_space = pl.BlockSpec(memory_space=pl.ANY)
+    vmem = pl.BlockSpec(memory_space=pltpu.VMEM)
+    cols = BAND_LAGS * COARSE
+    rows = SUBBANDS * COARSE
+    planes, key = pl.pallas_call(
+        planes_kernel,
+        out_shape=(
+            jax.ShapeDtypeStruct((SUBBANDS, 5, COARSE, SAMPLE_LANES), jnp.bfloat16),
+            jax.ShapeDtypeStruct((trials, rows), jnp.bfloat16),
+        ),
+        in_specs=[any_space] * 4,
+        out_specs=(vmem, vmem),
+        scratch_shapes=[
+            pltpu.VMEM((span, beams, chans), jnp.bfloat16),
+            pltpu.VMEM((COARSE, chans), jnp.int32),
+            pltpu.VMEM((SUBBANDS, trials), jnp.int32),
+            pltpu.VMEM((1, trials), jnp.int32),
+            pltpu.VMEM((chans, cols), jnp.bfloat16),
+            pltpu.VMEM(((span + 2) * beams, cols), jnp.float32),
+            pltpu.VMEM((chips, 5, COARSE, SAMPLE_LANES), jnp.bfloat16),
+            pltpu.VMEM((SUBBANDS, 5, COARSE, SAMPLE_LANES), jnp.bfloat16),
+            pltpu.SemaphoreType.DMA((span // CHUNK_TIMES,)),
+            pltpu.SemaphoreType.DMA((3,)),
+            pltpu.SemaphoreType.DMA((chips,)),
+            pltpu.SemaphoreType.DMA((chips,)),
+            pltpu.SemaphoreType.DMA((chips,)),
+            pltpu.SemaphoreType.DMA((chips,)),
+        ],
+        compiler_params=pltpu.CompilerParams(
+            collective_id=0, has_side_effects=True, vmem_limit_bytes=40 * 2**20
+        ),
+        cost_estimate=pl.CostEstimate(
+            flops=2 * span * beams * chans * cols,
+            bytes_accessed=2 * span * beams * chans,
+            transcendentals=0,
+        ),
+    )(
+        jnp.transpose(intensities, (2, 0, 1)),
+        sweep_delays.T,
+        band_offsets,
+        coarse_trial[None, :],
+    )
+    return pl.pallas_call(
+        trials_kernel,
+        out_shape=jax.ShapeDtypeStruct((trials, 2, 2 * SAMPLE_LANES), jnp.float32),
+        in_specs=[vmem, vmem],
+        out_specs=vmem,
+        scratch_shapes=[pltpu.VMEM((2, SUB_LAGS * rows, 2 * SAMPLE_LANES), jnp.bfloat16)],
+        compiler_params=pltpu.CompilerParams(vmem_limit_bytes=32 * 2**20),
+        cost_estimate=pl.CostEstimate(
+            flops=4 * trials * SUB_LAGS * rows * 2 * SAMPLE_LANES,
+            bytes_accessed=16 * trials * SAMPLE_LANES,
+            transcendentals=0,
+        ),
+    )(planes, key)
+
+
+def program(intensities, sweep_delays, band_offsets, coarse_trial):
+    beams, chans, span = intensities.shape
+    chips, cores = lax.axis_size("beam"), lax.axis_size("sub")
+    one_band = (
+        chans == CHANNELS // SUBBANDS
+        and cores == 2
+        and chips * cores == SUBBANDS
+        and beams == 2 * chips
+        and beams == 16
+        and span == 2 * SAMPLE_LANES + BAND_LAGS + SUB_LAGS - 2
+        and span % CHUNK_TIMES == 0
+    )
+    chosen = on_device_fused if one_band else on_device
+    return chosen(intensities, sweep_delays, band_offsets, coarse_trial)
+
+
 def solution(mesh):
     in_specs = (P("groups", ("beam", "sub"), None), P(), P(), P())
     out_specs = P("sub", ("groups", "beam"), None)
     return jax.shard_map(
-        on_device, mesh=mesh, in_specs=in_specs, out_specs=out_specs, check_vma=False
-    )
+        program, mesh=mesh, in_specs=in_specs, out_specs=out_specs, check_vma=False
+    )

time: 73.5 us -> 29.6 us (0.40)
  Pallas kernels: 0 us -> 23.1 us
  matrix products: 20.1 us -> 0 us
  waiting for transfers between devices: 15.7 us -> 0 us
  between operations: 13.6 us -> 0.01 us
  other arithmetic: 8.99 us -> 0 us
  starting transfers between devices: 7.32 us -> 0 us
  local copies, waits for them, and re-layouts: 7.37 us -> 6.26 us
    pallas_call x0 -> x2, Pallas kernels: none -> 23.1 us  [the longest x1 20.6 us: on_device_fused(): pl.pallas_call(planes_kernel, out_shape=(jax.ShapeDtypeStruct((SUBBANDS,...]
    dot_general x10 -> x0, matrix products: 20.1 us -> none  [the longest x1 13.4 us: add_block(): jnp.einsum('bct,cn->btn', intens, table, preferred_element_type=jnp.float32)]
    reduce_scatter x1 -> x0, waiting for transfers between devices: 8.82 us -> none  [on_device(): lax.psum_scatter(section_two(rounded[None], band_offsets, coarse_trial, l...]
    all_to_all x1 -> x0, starting transfers between devices: 7.28 us -> none  [on_device(): lax.all_to_all(grouped, 'beam', split_axis=0, concat_axis=0, tiled=True)]
    all_to_all x1 -> x0, waiting for transfers between devices: 6.9 us -> none  [on_device(): lax.all_to_all(grouped, 'beam', split_axis=0, concat_axis=0, tiled=True)]
    add x1 -> x0, other arithmetic: 4.15 us -> none  [section_one(): result = result + spread[:, lag:lag + span_out, lag * cols:(lag + 1) * cols]]
    unnamed x14 -> x8, local copies, waits for them, and re-layouts: 2.61 us -> 6.26 us
    unnamed x5 -> x0, other arithmetic: 3.39 us -> none
  transfers between devices with their start and end apart: 2 -> 0, of which waited for: 2 -> 0; matrix products, arithmetic and copies ran while one was open for 6% -> 0% of each run, Pallas kernels for 0% -> 0%
where the time goes in v1:
time: 29.6 us; the launch traced here: 29.4 us
  Pallas kernels  23.1 us (78%)
  local copies, waits for them, and re-layouts  6.26 us (21%)
    pallas_call x1, Pallas kernels, on_device_fused(): pl.pallas_call(planes_kernel, out_shape=(jax.ShapeDtypeStruct((SUBBANDS,...  20.6 us
    unnamed x8, local copies, waits for them, and re-layouts  6.26 us
    pallas_call x1, Pallas kernels, on_device_fused(): pl.pallas_call(trials_kernel, out_shape=jax.ShapeDtypeStruct((trials, 2,...  2.49 us

profile of v1, /device:TPU:0, one launch (start us, length us, event | category | flops | bytes accessed | tf_op | source)
XLA Modules:
  0.0 29.4 jit_solution(2581451428275356374)
XLA Ops:
  0.0 0.0 copy-start
  0.0 3.5 %copy-done = bf16[16,1024,270]{1,0,2:T(8,128)(2,1)S(1)} copy-done((bf16[16,1024,270]{1,0,2:T(8,128)(2,1)S(1)}, bf16[16,1024,270]{1,0,2:T(8,128)(2,1)}, u32[]{:S(2)}) %copy-start) | copy-done | bytes 8847384
  3.5 0.0 copy-start.1
  3.5 1.2 %copy-done.1 = s32[16384,16]{0,1:T(8,128)S(1)} copy-done((s32[16384,16]{0,1:T(8,128)S(1)}, s32[16384,16]{0,1:T(8,128)}, u32[]{:S(2)}) %copy-start.1) | copy-done | bytes 1048600
  4.7 0.0 copy-start.2
  4.7 0.8 %copy-done.2 = s32[16,1024]{1,0:T(8,128)S(1)} copy-done((s32[16,1024]{1,0:T(8,128)S(1)}, s32[16,1024]{1,0:T(8,128)}, u32[]{:S(2)}) %copy-start.2) | copy-done | bytes 65560
  5.6 0.0 copy-start.3
  5.6 0.7 %copy-done.3 = s32[1024]{0:T(1024)S(1)} copy-done((s32[1024]{0:T(1024)S(1)}, s32[1024]{0:T(1024)}, u32[]{:S(2)}) %copy-start.3) | copy-done | bytes 4120
  6.3 20.6 %shard_map.46 = (bf16[16,5,16,128]{3,2,1,0:T(8,128)(2,1)S(1)}, bf16[512,256]{1,0:T(8,128)(2,1)S(1)}) custom-call(bf16[270,16,1024]{2,1,0:T(8,128)(2,1)S(1)} %bitcast.3, s32[16,16384]{1,0:T(8,128)S(1)} %bitcast.4, s32[16,1024]{1,0:T(8,128)S(1)} %copy-done.2, s32[1,1024]{1,0:T(1,128)S(1)} %bitcast.5), custom_call_target="tpu_custom_call" | custom-call | flops 1132462080 | bytes 8847360 | tf_op jit(solution)/shard_map/pallas_call | solution.py:298
  26.9 2.5 %shard_map.47 = f32[512,2,256]{2,1,0:T(2,128)} custom-call(bf16[16,5,16,128]{3,2,1,0:T(8,128)(2,1)S(1)} %get-tuple-element.7.planes, bf16[512,256]{1,0:T(8,128)(2,1)S(1)} %get-tuple-element.8.key), custom_call_target="tpu_custom_call" | custom-call | flops 1073741824 | bytes 1048576 | tf_op jit(solution)/shard_map/pallas_call | solution.py:336
Async XLA Ops:
  0.0 3.5 %copy-start = (bf16[16,1024,270]{1,0,2:T(8,128)(2,1)S(1)}, bf16[16,1024,270]{1,0,2:T(8,128)(2,1)}, u32[]{:S(2)}) copy-start(bf16[16,1024,270]{1,0,2:T(8,128)(2,1)} %param.4) | copy-start | bytes 26542084
  3.5 1.2 %copy-start.1 = (s32[16384,16]{0,1:T(8,128)S(1)}, s32[16384,16]{0,1:T(8,128)}, u32[]{:S(2)}) copy-start(s32[16384,16]{0,1:T(8,128)} %param.5) | copy-start | bytes 3145732
  4.7 0.8 %copy-start.2 = (s32[16,1024]{1,0:T(8,128)S(1)}, s32[16,1024]{1,0:T(8,128)}, u32[]{:S(2)}) copy-start(s32[16,1024]{1,0:T(8,128)} %offsets_hbm.1) | copy-start | bytes 196612
  5.6 0.7 %copy-start.3 = (s32[1024]{0:T(1024)S(1)}, s32[1024]{0:T(1024)}, u32[]{:S(2)}) copy-start(s32[1024]{0:T(1024)} %param.7) | copy-start | bytes 12292

commit v2 on v1

--- a/solution.py
+++ b/solution.py
@@ -95,6 +95,7 @@
 
 SAMPLE_LANES = 128
 CHUNK_TIMES = 30
+CHOOSE_TIMES = 10
 
 
 def planes_kernel(
@@ -110,8 +111,11 @@
     coarse_vmem,
     table,
     spread,
-    send,
-    recv,
+    chosen,
+    send_low,
+    send_high,
+    recv_low,
+    recv_high,
     x_sem,
     small_sem,
     send_sem,
@@ -120,12 +124,15 @@
     pass_recv_sem,
 ):
     span, beams, chans = x_vmem.shape
-    chips = send.shape[0]
+    chips = send_low.shape[0]
     trials = offsets_vmem.shape[1]
     chunks = span // CHUNK_TIMES
+    times = chosen.shape[0] // beams
+    cols = BAND_LAGS * COARSE
     me = lax.axis_index("beam")
     core = lax.axis_index("sub")
     mesh_id = pl.DeviceIdType.MESH
+    sends, recvs = (send_low, send_high), (recv_low, recv_high)
 
     def load_chunk(index):
         part = pl.ds(index * CHUNK_TIMES, CHUNK_TIMES)
@@ -154,90 +161,110 @@
     delays = delays_vmem[...]
     hits = [(delays == lag).astype(jnp.float32) for lag in range(BAND_LAGS)]
     table[...] = jnp.concatenate(hits, axis=0).T.astype(jnp.bfloat16)
-    spread[span * beams :, :] = jnp.zeros((spread.shape[0] - span * beams, spread.shape[1]), jnp.float32)
-
-    def multiply(index, carry):
-        load_chunk(index).wait()
-        rows = CHUNK_TIMES * beams
-        block = x_vmem[pl.ds(index * CHUNK_TIMES, CHUNK_TIMES)].reshape(rows, chans)
-        spread[pl.ds(pl.multiple_of(index * rows, rows), rows), :] = jnp.dot(
+    spread[span * beams :, :] = jnp.zeros((spread.shape[0] - span * beams, cols), jnp.float32)
+    rows = CHUNK_TIMES * beams
+
+    def multiply(index):
+        block = x_vmem[index * CHUNK_TIMES : (index + 1) * CHUNK_TIMES].reshape(rows, chans)
+        spread[index * rows : (index + 1) * rows, :] = jnp.dot(
             block, table[...], preferred_element_type=jnp.float32
         )
-        return carry
-
-    lax.fori_loop(0, chunks, multiply, 0)
-
-    def lagged(beam, start, count):
-        lane_lag = lax.broadcasted_iota(jnp.int32, (count, BAND_LAGS * COARSE), 1) // COARSE
-        total = spread[pl.ds(beam + beams * start, count, stride=beams), :]
-        for lag in range(1, BAND_LAGS):
-            later = spread[pl.ds(beam + beams * (start + lag), count, stride=beams), :]
-            total = jnp.where(lane_lag == lag, later, total)
-        return total
-
-    def folded(rows):
-        turned = rows.T
+
+    def choose(start, stop):
+        for low in range(start, stop, CHOOSE_TIMES):
+            count = min(CHOOSE_TIMES, stop - low)
+            value = spread[low * beams : (low + count + BAND_LAGS - 1) * beams, :]
+            for bit in (1, 2, 4):
+                size = value.shape[0] - bit * beams
+                lane_lag = lax.broadcasted_iota(jnp.int32, (size, cols), 1) // COARSE
+                value = jnp.where(lane_lag & bit != 0, value[bit * beams :], value[:size])
+            chosen[low * beams : (low + count) * beams, :] = value
+
+    def folded(part):
+        turned = part.T
         total = turned[0:COARSE]
         for lag in range(1, BAND_LAGS):
             total = total + turned[lag * COARSE : (lag + 1) * COARSE]
         return total.astype(jnp.bfloat16)
 
-    def beam_pair(chip):
-        low = chip * 2
-        blocks = []
-        for beam in (low, low + 1):
-            for start in (0, SAMPLE_LANES):
-                blocks.append(folded(lagged(beam, start, SAMPLE_LANES)))
-        ends = [lagged(beam, 2 * SAMPLE_LANES, 8) for beam in (low, low + 1)]
-        ends.append(jnp.zeros((SAMPLE_LANES - 16, BAND_LAGS * COARSE), jnp.float32))
-        blocks.append(folded(jnp.concatenate(ends, axis=0)))
-        return blocks
-
-    def send_copy(step):
+    def half_block(beam, start):
+        return folded(chosen[pl.ds(beam + beams * start, SAMPLE_LANES, stride=beams), :])
+
+    def send_copy(part, step):
         peer = lax.rem(me + step, chips)
         return pltpu.make_async_remote_copy(
-            src_ref=send.at[peer],
-            dst_ref=recv.at[me * 2 + core],
-            send_sem=send_sem.at[step],
-            recv_sem=recv_sem.at[me],
+            src_ref=sends[part].at[peer],
+            dst_ref=recvs[part].at[me * 2 + core],
+            send_sem=send_sem.at[part, step],
+            recv_sem=recv_sem.at[part, me],
             device_id={"beam": peer, "sub": core},
             device_id_type=mesh_id,
         )
 
-    def arrival(source):
+    def arrival(part, source):
         return pltpu.make_async_remote_copy(
-            src_ref=send.at[source],
-            dst_ref=recv.at[source * 2 + core],
-            send_sem=send_sem.at[0],
-            recv_sem=recv_sem.at[source],
+            src_ref=sends[part].at[source],
+            dst_ref=recvs[part].at[source * 2 + core],
+            send_sem=send_sem.at[part, 0],
+            recv_sem=recv_sem.at[part, source],
             device_id={"beam": source, "sub": core},
             device_id_type=mesh_id,
         )
 
-    def pass_copy(source, side):
-        slot = recv.at[source * 2 + side]
+    def pass_copy(part, source, side):
+        slot = recvs[part].at[source * 2 + side]
         return pltpu.make_async_remote_copy(
             src_ref=slot,
             dst_ref=slot,
-            send_sem=pass_send_sem.at[source],
-            recv_sem=pass_recv_sem.at[source],
+            send_sem=pass_send_sem.at[part, source],
+            recv_sem=pass_recv_sem.at[part, source],
             device_id={"beam": me, "sub": 1 - core},
             device_id_type=mesh_id,
         )
 
-    pl.semaphore_wait(barrier, chips)
-
-    def send_pair(step, carry):
-        peer = lax.rem(me + step, chips)
-        for index, block in enumerate(beam_pair(peer)):
-            send[peer, index] = block
-        send_copy(step).start()
-        return carry
-
-    lax.fori_loop(1, chips, send_pair, 0)
-    for index, block in enumerate(beam_pair(me)):
-        recv[me * 2 + core, index] = block
-    pass_copy(me, core).start()
+    def send_part(part, ends):
+        start = part * SAMPLE_LANES
+
+        def send_pair(step, carry):
+            peer = lax.rem(me + step, chips)
+            for beam in range(2):
+                sends[part][peer, beam] = half_block(peer * 2 + beam, start)
+            if ends is not None:
+                sends[part][peer, 2] = ends
+            send_copy(part, step).start()
+            return carry
+
+        lax.fori_loop(1, chips, send_pair, 0)
+        for beam in range(2):
+            recvs[part][me * 2 + core, beam] = half_block(me * 2 + beam, start)
+        if ends is not None:
+            recvs[part][me * 2 + core, 2] = ends
+        pass_copy(part, me, core).start()
+
+    def pass_on(part):
+        for step in range(1, chips):
+            source = lax.rem(me + chips - step, chips)
+            arrival(part, source).wait_recv()
+            pass_copy(part, source, core).start()
+
+    done = 0
+    sent = False
+    for index in range(chunks + 1):
+        if index < chunks:
+            load_chunk(index).wait()
+            multiply(index)
+        if index:
+            ready = times if index == chunks else index * CHUNK_TIMES - BAND_LAGS + 1
+            choose(done, ready)
+            done = ready
+        if not sent and done >= SAMPLE_LANES:
+            sent = True
+            pl.semaphore_wait(barrier, chips)
+            send_part(0, None)
+    ends = [
+        chosen[pl.ds(beam + 2 * SAMPLE_LANES * beams, 8, stride=beams), :] for beam in range(beams)
+    ]
+    send_part(1, folded(jnp.concatenate(ends, axis=0)))
 
     offset_copy.wait()
     coarse_copy.wait()
@@ -250,25 +277,27 @@
     ]
     key_out[...] = jnp.concatenate(keys, axis=0).T.astype(jnp.bfloat16)
 
-    for step in range(1, chips):
-        source = lax.rem(me + chips - step, chips)
-        arrival(source).wait_recv()
-        pass_copy(source, core).start()
-    for step in range(chips):
-        source = lax.rem(me + chips - step, chips)
-        pass_copy(source, 1 - core).wait_recv()
-    for step in range(1, chips):
-        send_copy(step).wait_send()
-    for step in range(chips):
-        source = lax.rem(me + chips - step, chips)
-        pass_copy(source, core).wait_send()
-    planes_out[...] = recv[...]
+    pass_on(0)
+    pass_on(1)
+    for part in range(2):
+        for step in range(chips):
+            source = lax.rem(me + chips - step, chips)
+            pass_copy(part, source, 1 - core).wait_recv()
+    for index, (part, place) in enumerate(((0, 0), (1, 0), (0, 1), (1, 1), (1, 2))):
+        planes_out[:, index] = recvs[part][:, place]
+    for part in range(2):
+        for step in range(1, chips):
+            send_copy(part, step).wait_send()
+        for step in range(chips):
+            source = lax.rem(me + chips - step, chips)
+            pass_copy(part, source, core).wait_send()
 
 
 def trials_kernel(planes, key, out, shifted):
     rows = SUBBANDS * COARSE
     trials = key.shape[0]
     samples = 2 * SAMPLE_LANES
+    me = lax.axis_index("beam")
     keys = key[...]
     one, zero = jnp.bfloat16(1), jnp.bfloat16(0)
     table = jnp.concatenate(
@@ -278,9 +307,9 @@
         parts = [planes[:, 2 * beam + index].reshape(rows, SAMPLE_LANES) for index in range(2)]
         end = planes[:, 4].reshape(rows, SAMPLE_LANES)
         whole = jnp.concatenate(parts + [end], axis=1).astype(jnp.float32)
-        if beam:
-            turned = pltpu.roll(whole[:, samples:], SAMPLE_LANES - 8 * beam, 1)
-            whole = jnp.concatenate([whole[:, :samples], turned], axis=1)
+        back = lax.rem(SAMPLE_LANES - 8 * (2 * me + beam), SAMPLE_LANES)
+        turned = pltpu.roll(whole[:, samples:], back, 1)
+        whole = jnp.concatenate([whole[:, :samples], turned], axis=1)
         for lag in range(SUB_LAGS):
             moved = whole if lag == 0 else pltpu.roll(whole, whole.shape[1] - lag, 1)
             shifted[beam, lag * rows : (lag + 1) * rows, :] = moved[:, :samples].astype(jnp.bfloat16)
@@ -310,17 +339,20 @@
             pltpu.VMEM((1, trials), jnp.int32),
             pltpu.VMEM((chans, cols), jnp.bfloat16),
             pltpu.VMEM(((span + 2) * beams, cols), jnp.float32),
-            pltpu.VMEM((chips, 5, COARSE, SAMPLE_LANES), jnp.bfloat16),
-            pltpu.VMEM((SUBBANDS, 5, COARSE, SAMPLE_LANES), jnp.bfloat16),
+            pltpu.VMEM(((2 * SAMPLE_LANES + 8) * beams, cols), jnp.float32),
+            pltpu.VMEM((chips, 2, COARSE, SAMPLE_LANES), jnp.bfloat16),
+            pltpu.VMEM((chips, 3, COARSE, SAMPLE_LANES), jnp.bfloat16),
+            pltpu.VMEM((SUBBANDS, 2, COARSE, SAMPLE_LANES), jnp.bfloat16),
+            pltpu.VMEM((SUBBANDS, 3, COARSE, SAMPLE_LANES), jnp.bfloat16),
             pltpu.SemaphoreType.DMA((span // CHUNK_TIMES,)),
             pltpu.SemaphoreType.DMA((3,)),
-            pltpu.SemaphoreType.DMA((chips,)),
-            pltpu.SemaphoreType.DMA((chips,)),
-            pltpu.SemaphoreType.DMA((chips,)),
-            pltpu.SemaphoreType.DMA((chips,)),
+            pltpu.SemaphoreType.DMA((2, chips)),
+            pltpu.SemaphoreType.DMA((2, chips)),
+            pltpu.SemaphoreType.DMA((2, chips)),
+            pltpu.SemaphoreType.DMA((2, chips)),
         ],
         compiler_params=pltpu.CompilerParams(
-            collective_id=0, has_side_effects=True, vmem_limit_bytes=40 * 2**20
+            collective_id=0, has_side_effects=True, vmem_limit_bytes=62 * 2**20
         ),
         cost_estimate=pl.CostEstimate(
             flops=2 * span * beams * chans * cols,
@@ -339,7 +371,7 @@
         in_specs=[vmem, vmem],
         out_specs=vmem,
         scratch_shapes=[pltpu.VMEM((2, SUB_LAGS * rows, 2 * SAMPLE_LANES), jnp.bfloat16)],
-        compiler_params=pltpu.CompilerParams(vmem_limit_bytes=32 * 2**20),
+        compiler_params=pltpu.CompilerParams(vmem_limit_bytes=62 * 2**20),
         cost_estimate=pl.CostEstimate(
             flops=4 * trials * SUB_LAGS * rows * 2 * SAMPLE_LANES,
             bytes_accessed=16 * trials * SAMPLE_LANES,

time: 29.6 us -> 23.4 us (0.79)
  local copies, waits for them, and re-layouts: 6.26 us -> 0 us
    unnamed x8 -> x0, local copies, waits for them, and re-layouts: 6.26 us -> none
    pallas_call x1, Pallas kernels: 2.49 us -> 3.52 us  [on_device_fused(): pl.pallas_call(trials_kernel, out_shape=jax.ShapeDtypeStruct((trials, 2,...]
    pallas_call x1, Pallas kernels: 20.6 us -> 19.7 us  [on_device_fused(): pl.pallas_call(planes_kernel, out_shape=(jax.ShapeDtypeStruct((SUBBANDS,...]
where the time goes in v2:
time: 23.4 us; the launch traced here: 23.2 us
  Pallas kernels  23.2 us (99%)
    pallas_call x1, Pallas kernels, on_device_fused(): pl.pallas_call(planes_kernel, out_shape=(jax.ShapeDtypeStruct((SUBBANDS,...  19.7 us
    pallas_call x1, Pallas kernels, on_device_fused(): pl.pallas_call(trials_kernel, out_shape=jax.ShapeDtypeStruct((trials, 2,...  3.52 us

profile of v2, /device:TPU:0, one launch (start us, length us, event | category | flops | bytes accessed | tf_op | source)
XLA Modules:
  0.0 23.2 jit_solution(1468305979450531160)
XLA Ops:
  0.0 19.7 %shard_map.46 = (bf16[16,5,16,128]{3,2,1,0:T(8,128)(2,1)}, bf16[512,256]{1,0:T(8,128)(2,1)}) custom-call(bf16[270,16,1024]{2,1,0:T(8,128)(2,1)} %bitcast.3, s32[16,16384]{1,0:T(8,128)} %bitcast.4, s32[16,1024]{1,0:T(8,128)} %offsets_hbm.1, s32[1,1024]{1,0:T(1,128)} %bitcast.5), custom_call_target="tpu_custom_call" | custom-call | flops 1132462080 | bytes 8847360 | tf_op jit(solution)/shard_map/pallas_call | solution.py:327
  19.7 3.5 %shard_map.47 = f32[512,2,256]{2,1,0:T(2,128)} custom-call(bf16[16,5,16,128]{3,2,1,0:T(8,128)(2,1)} %get-tuple-element.7.planes, bf16[512,256]{1,0:T(8,128)(2,1)} %get-tuple-element.8.key), custom_call_target="tpu_custom_call" | custom-call | flops 1073741824 | bytes 1048576 | tf_op jit(solution)/shard_map/pallas_call | solution.py:368

commit v3 on v2

--- a/solution.py
+++ b/solution.py
@@ -94,7 +94,7 @@
 
 
 SAMPLE_LANES = 128
-CHUNK_TIMES = 30
+CHUNK_TIMES = 54
 CHOOSE_TIMES = 10
 
 

time: 23.4 us -> 21.8 us (0.932)
  Pallas kernels: 23.2 us -> 21.7 us
    pallas_call x1, Pallas kernels: 19.7 us -> 18.1 us  [on_device_fused(): pl.pallas_call(planes_kernel, out_shape=(jax.ShapeDtypeStruct((SUBBANDS,...]
where the time goes in v3:
time: 21.8 us; the launch traced here: 21.7 us
  Pallas kernels  21.7 us (100%)
    pallas_call x1, Pallas kernels, on_device_fused(): pl.pallas_call(planes_kernel, out_shape=(jax.ShapeDtypeStruct((SUBBANDS,...  18.1 us
    pallas_call x1, Pallas kernels, on_device_fused(): pl.pallas_call(trials_kernel, out_shape=jax.ShapeDtypeStruct((trials, 2,...  3.52 us

profile of v3, /device:TPU:0, one launch (start us, length us, event | category | flops | bytes accessed | tf_op | source)
XLA Modules:
  0.0 21.7 jit_solution(11454894119431889746)
XLA Ops:
  0.0 18.1 %shard_map.46 = (bf16[16,5,16,128]{3,2,1,0:T(8,128)(2,1)}, bf16[512,256]{1,0:T(8,128)(2,1)}) custom-call(bf16[270,16,1024]{2,1,0:T(8,128)(2,1)} %bitcast.3, s32[16,16384]{1,0:T(8,128)} %bitcast.4, s32[16,1024]{1,0:T(8,128)} %offsets_hbm.1, s32[1,1024]{1,0:T(1,128)} %bitcast.5), custom_call_target="tpu_custom_call" | custom-call | flops 1132462080 | bytes 8847360 | tf_op jit(solution)/shard_map/pallas_call | solution.py:327
  18.1 3.5 %shard_map.47 = f32[512,2,256]{2,1,0:T(2,128)} custom-call(bf16[16,5,16,128]{3,2,1,0:T(8,128)(2,1)} %get-tuple-element.7.planes, bf16[512,256]{1,0:T(8,128)(2,1)} %get-tuple-element.8.key), custom_call_target="tpu_custom_call" | custom-call | flops 1073741824 | bytes 1048576 | tf_op jit(solution)/shard_map/pallas_call | solution.py:368
